TPU v7x, 32 devices: a whole 2x2x4 slice. The times are simulated.
32 devices in a mesh: qry: 8 (over z, core), lib: 4 (over y, x).
Axes of the slice: x: 2, y: 2, z: 4, core: 2. Of those that a mesh axis runs over, the one named last changes fastest.
Arguments:
- query_prints: bfloat16 [256, 2048], P('qry'), may hold values from -500 to 500, as said below
- library_prints: bfloat16 [24576, 2048], P(('lib', 'qry')), may hold values from -1500 to 1500
- query_atoms: float32 [256, 192], P(('qry', 'lib')), may hold values from -3 to 3, as said below
- conformer_atoms: float32 [24576, 192], P(('lib', 'qry')), may hold values from -3 to 3, as said below
- candidates: int32 [256, 64], P(('qry', 'lib')), may hold values from 0 to 24575, as said below
- candidate_count: int32 [256], P(('qry', 'lib')), may hold values from 16 to 64
- home_row: int32 [24576], replicated, may hold values from 0 to 24575, as said below
Outputs:
- tversky: bfloat16 [256, 24576], P(None, ('lib', 'qry'))
- rescore: float32 [256, 64], P(('qry', 'lib'))
Inputs may be any that keep to these rules, and one draw needn't show every extreme that they name: query_prints rows and columns carry independent positive scales. `query_atoms`: each row holds x, y and z of 48 atom slots, then their weights; a padded slot has weight 0, and every row has at least one atom of positive weight. `conformer_atoms`: each row holds x, y and z of 48 atom slots, then their weights; a padded slot has weight 0, and every row has at least one atom of positive weight. Among the candidates in the rows of one device (8 queries, padding included), at most 36 have storage rows in any one block of rows b * 768 to (b + 1) * 768 - 1; in every draw some such block receives exactly 36 from the rows of every device. `home_row`: a permutation of 0 to 24575.
All inputs are finite; a program needn't handle non-finite values.
Results may differ from a plain program's by a relative error of at most 0.0029.
Values may be sent and summed in bfloat16 or wider, within the bound.
A program may use at most 64 MiB of HBM per device.

v0:
```python
import jax
import jax.numpy as jnp
from jax import lax
from jax.sharding import PartitionSpec as P

SHARPNESS = 0.8
EPSILON = 1e-06


def screen_rows(piece, library):
    scores = lax.dot_general(
        piece, library, (((1,), (1,)), ((), ())), preferred_element_type=jnp.float32
    )
    norms = jnp.sum(jnp.square(piece.astype(jnp.float32)), axis=1, keepdims=True)
    return (scores / (norms + EPSILON)).astype(jnp.bfloat16)


def selector(indices, rows):
    return (jnp.arange(rows, dtype=jnp.int32)[:, None] == indices[None, :]).astype(jnp.float32)


def pick_columns(table, indices):
    picks = selector(indices, table.shape[0])
    columns = lax.dot_general(
        table,
        picks,
        (((0,), (0,)), ((), ())),
        precision=lax.Precision.HIGHEST,
        preferred_element_type=jnp.float32,
    )
    return columns.reshape(4, -1, indices.shape[0])


def pick_rows(table, indices):
    picks = selector(indices, table.shape[0])
    return lax.dot_general(
        picks,
        table,
        (((0,), (0,)), ((), ())),
        precision=lax.Precision.HIGHEST,
        preferred_element_type=jnp.float32,
    )


def to_atoms(flat):
    return flat.reshape(flat.shape[0], 4, -1).transpose(1, 2, 0)


def intersection(first, second):
    dist = jnp.square(first[0][:, None, :] - second[0][None, :, :])
    dist = dist + jnp.square(first[1][:, None, :] - second[1][None, :, :])
    dist = dist + jnp.square(first[2][:, None, :] - second[2][None, :, :])
    return jnp.sum(
        first[3][:, None, :] * second[3][None, :, :] * jnp.exp(-SHARPNESS * dist), axis=(0, 1)
    )


def body(
    query_prints,
    library_prints,
    query_atoms,
    conformer_atoms,
    candidates,
    candidate_count,
    home_row,
):
    query_groups = lax.axis_size("qry")
    library_groups = lax.axis_size("lib")
    devices = query_groups * library_groups
    own_rows = library_prints.shape[0]
    local_queries = query_atoms.shape[0]
    listed = candidates.shape[1]
    pairs = local_queries * listed
    capacity = 2 * ((pairs + devices - 1) // devices) + 4
    tversky = screen_rows(lax.all_gather(query_prints, "qry", axis=0, tiled=True), library_prints)
    stored = jnp.take(home_row, candidates.reshape(-1), axis=0)
    owner = stored // own_rows
    slot_index = stored - owner * own_rows
    first_query = (lax.axis_index("qry") * library_groups + lax.axis_index("lib")) * local_queries
    query_index = first_query + jnp.arange(pairs, dtype=jnp.int32) // listed
    position = jnp.arange(pairs, dtype=jnp.int32)
    earlier = position[:, None] > position[None, :]
    same_owner = owner[:, None] == owner[None, :]
    rank = jnp.sum((earlier & same_owner).astype(jnp.int32), axis=1)
    target = owner * capacity + rank
    bucket_shape = (library_groups, query_groups, capacity)
    send_slot = (
        jnp.zeros(devices * capacity, jnp.int32).at[target].set(slot_index).reshape(bucket_shape)
    )
    send_query = (
        jnp.zeros(devices * capacity, jnp.int32).at[target].set(query_index).reshape(bucket_shape)
    )
    got_slot, got_query = (
        lax.all_to_all(
            lax.all_to_all(send_slot, "qry", split_axis=1, concat_axis=1, tiled=True),
            "lib",
            split_axis=0,
            concat_axis=0,
            tiled=True,
        ),
        lax.all_to_all(
            lax.all_to_all(send_query, "qry", split_axis=1, concat_axis=1, tiled=True),
            "lib",
            split_axis=0,
            concat_axis=0,
            tiled=True,
        ),
    )
    flat_slots = got_slot.reshape(-1)
    fetched = pick_rows(conformer_atoms, flat_slots).reshape(
        library_groups, query_groups, capacity, -1
    )
    prior_all = tversky[got_query.reshape(-1), flat_slots].astype(jnp.float32).reshape(bucket_shape)
    back_atoms, back_prior = (
        lax.all_to_all(
            lax.all_to_all(
                fetched.astype(jnp.bfloat16), "qry", split_axis=1, concat_axis=1, tiled=True
            ),
            "lib",
            split_axis=0,
            concat_axis=0,
            tiled=True,
        ).astype(fetched.dtype),
        lax.all_to_all(
            lax.all_to_all(
                prior_all.astype(jnp.bfloat16), "qry", split_axis=1, concat_axis=1, tiled=True
            ),
            "lib",
            split_axis=0,
            concat_axis=0,
            tiled=True,
        ).astype(prior_all.dtype),
    )
    conformer = pick_columns(back_atoms.reshape(devices * capacity, -1), target)
    fragment = jnp.repeat(to_atoms(query_atoms), listed, axis=2)
    pair_cross = intersection(fragment, conformer)
    pair_self = intersection(conformer, conformer)
    pair_prior = back_prior.reshape(-1)[target]
    own_atoms = to_atoms(query_atoms)
    query_self = jnp.repeat(intersection(own_atoms, own_atoms), listed)
    shape = pair_cross / (query_self + pair_self - pair_cross)
    live = jnp.arange(listed, dtype=jnp.int32)[None, :] < candidate_count[:, None]
    rescore = jnp.where(live, (shape + pair_prior).reshape(local_queries, listed), 0.0)
    return (tversky, rescore)


def solution(mesh):
    return jax.shard_map(
        body,
        mesh=mesh,
        in_specs=(
            P("qry", None),
            P(("lib", "qry"), None),
            P(("qry", "lib"), None),
            P(("lib", "qry"), None),
            P(("qry", "lib"), None),
            P(("qry", "lib")),
            P(),
        ),
        out_specs=(P(None, ("lib", "qry")), P(("qry", "lib"), None)),
        check_vma=False,
    )
```

profile of v0, /device:TPU:0, one launch (start us, length us, event | category | flops | bytes accessed | tf_op | source)
XLA Modules:
  0.0 148.4 jit_solution(1439643963473406378)
XLA Ops:
  8.9 3.6 %gather_fusion = s32[512]{0:T(512)S(1)} fusion(s32[24576]{0:T(1024)} %param.13, s32[1024]{0:T(1024)S(1)} %pad_clamp_fusion.1), kind=kCustom, calls=%fused_computation | custom fusion | bytes 6144 | tf_op jit(solution)/shard_map/jit(_take)/gather | solution.py:76
  12.8 2.5 %scatter_custom_fusion = s32[1152]{0:T(1024)S(1)} fusion(s32[512]{0:T(512)S(1)} %bitcast.37, s32[512]{0:T(512)S(1)} %get-tuple-element.4, s32[]{:T(128)} %constant.31.clone.1), kind=kCustom, calls=%fused_computation.44 | custom fusion | bytes 4612 | tf_op jit(solution)/shard_map/scatter | solution.py:88
  16.1 6.3 %all-to-all-start = ((s32[8,1,144]{2,1,0:T(1,128)}), s32[8,1,144]{2,1,0:T(1,128)S(1)}, u32[]{:S(2)}, u32[]{:S(2)}) async-start(s32[8,1,144]{2,1,0:T(1,128)} %reshape.354), calls=%async_computation | async-start | bytes 16384 | tf_op jit(solution)/shard_map/all_to_all | solution.py:95
  23.1 4.9 %all-to-all-done = s32[8,1,144]{2,1,0:T(1,128)S(1)} async-done(((s32[8,1,144]{2,1,0:T(1,128)}), s32[8,1,144]{2,1,0:T(1,128)S(1)}, u32[]{:S(2)}, u32[]{:S(2)}) %all-to-all-start) | async-done | bytes 4640 | tf_op jit(solution)/shard_map/all_to_all | solution.py:95
  29.9 3.7 %all-to-all-start.1 = ((s32[4,1,288]{2,1,0:T(1,128)}), s32[4,1,288]{2,1,0:T(1,128)S(1)}, u32[]{:S(2)}, u32[]{:S(2)}) async-start(s32[4,1,288]{2,1,0:T(1,128)} %reshape.356), calls=%async_computation.1 | async-start | bytes 12288 | tf_op jit(solution)/shard_map/all_to_all | solution.py:94
  33.7 2.4 %scatter_custom_fusion.1 = s32[1152]{0:T(1024)S(1)} fusion(s32[512]{0:T(512)S(1)} %bitcast.38, s32[512]{0:T(512)S(1)} %fusion.19, s32[]{:T(128)} %constant.31.clone.1), kind=kCustom, calls=%fused_computation.42 | custom fusion | bytes 4612 | tf_op jit(solution)/shard_map/scatter | solution.py:91
  36.9 1.4 all-to-all-done.1
  38.3 3.3 %all-to-all-start.4 = ((s32[8,1,144]{2,1,0:T(1,128)}), s32[8,1,144]{2,1,0:T(1,128)S(1)}, u32[]{:S(2)}, u32[]{:S(2)}) async-start(s32[8,1,144]{2,1,0:T(1,128)} %reshape.358), calls=%async_computation.4 | async-start | bytes 16384 | tf_op jit(solution)/shard_map/all_to_all | solution.py:102
  42.6 3.4 %fusion.1 = bf16[1152,192]{0,1:T(8,128)(2,1)} fusion(f32[768,192]{0,1:T(8,128)} %param.10, s32[1152]{0:T(1024)S(1)} %eq.45), kind=kOutput, calls=%fused_computation.9 | convolution fusion | flops 2039537664 | bytes 1036800 | tf_op jit(solution)/shard_map/dot_general | solution.py:36
  46.0 2.1 %copy.98 = bf16[1152,192]{1,0:T(8,128)(2,1)} copy(bf16[1152,192]{0,1:T(8,128)(2,1)} %fusion.1) | data formatting | bytes 884736 | tf_op jit(solution)/shard_map/convert_element_type | solution.py:117
  48.0 2.1 %convert_element_type.26 = bf16[4,8,36,192]{3,2,1,0:T(8,128)(2,1)} reshape(bf16[1152,192]{1,0:T(8,128)(2,1)} %copy.98) | data formatting | bytes 884736 | tf_op jit(solution)/shard_map/convert_element_type | solution.py:117
  50.2 2.4 %copy.99 = bf16[4,8,36,192]{3,0,2,1:T(4,128)(2,1)} copy(bf16[4,8,36,192]{3,2,1,0:T(8,128)(2,1)} %convert_element_type.26) | data formatting | bytes 884736 | tf_op jit(solution)/shard_map/convert_element_type | solution.py:117
  52.5 5.0 %all-to-all-start.2 = ((bf16[4,8,36,192]{3,0,2,1:T(4,128)(2,1)}), bf16[4,8,36,192]{3,0,2,1:T(4,128)(2,1)}, u32[]{:S(2)}, u32[]{:S(2)}) async-start(bf16[4,8,36,192]{3,0,2,1:T(4,128)(2,1)} %copy.99), calls=%async_computation.2 | async-start | bytes 1179648 | tf_op jit(solution)/shard_map/all_to_all | solution.py:116
  58.0 0.9 multiply_reduce_fusion.3
  60.4 14.1 %all-to-all-done.2 = bf16[4,8,36,192]{3,0,2,1:T(4,128)(2,1)} async-done(((bf16[4,8,36,192]{3,0,2,1:T(4,128)(2,1)}), bf16[4,8,36,192]{3,0,2,1:T(4,128)(2,1)}, u32[]{:S(2)}, u32[]{:S(2)}) %all-to-all-start.2) | async-done | bytes 442400 | tf_op jit(solution)/shard_map/all_to_all | solution.py:116
  74.4 3.2 %all-to-all-start.5 = ((s32[4,1,288]{2,1,0:T(1,128)}), s32[4,1,288]{2,1,0:T(1,128)S(1)}, u32[]{:S(2)}, u32[]{:S(2)}) async-start(s32[4,1,288]{2,1,0:T(1,128)} %reshape.360), calls=%async_computation.5 | async-start | bytes 12288 | tf_op jit(solution)/shard_map/all_to_all | solution.py:101
  81.7 2.1 %copy.100 = bf16[4,8,36,192]{3,1,2,0:T(8,128)(2,1)} copy(bf16[4,8,36,192]{3,0,2,1:T(4,128)(2,1)} %all-to-all-done.2) | data formatting | bytes 884736 | tf_op jit(solution)/shard_map/all_to_all | solution.py:116
  83.8 4.2 %all-to-all-start.3 = ((bf16[4,8,36,192]{3,1,2,0:T(8,128)(2,1)}), bf16[4,8,36,192]{3,1,2,0:T(8,128)(2,1)}, u32[]{:S(2)}, u32[]{:S(2)}) async-start(bf16[4,8,36,192]{3,1,2,0:T(8,128)(2,1)} %copy.100), calls=%async_computation.3 | async-start | bytes 1179648 | tf_op jit(solution)/shard_map/all_to_all | solution.py:115
  89.0 7.8 %all-to-all-done.3 = bf16[4,8,36,192]{3,1,2,0:T(8,128)(2,1)} async-done(((bf16[4,8,36,192]{3,1,2,0:T(8,128)(2,1)}), bf16[4,8,36,192]{3,1,2,0:T(8,128)(2,1)}, u32[]{:S(2)}, u32[]{:S(2)}) %all-to-all-start.3) | async-done | bytes 442400 | tf_op jit(solution)/shard_map/all_to_all | solution.py:115
  96.8 2.0 %copy.101 = bf16[4,8,36,192]{3,2,1,0:T(8,128)(2,1)} copy(bf16[4,8,36,192]{3,1,2,0:T(8,128)(2,1)} %all-to-all-done.3) | data formatting | bytes 884736 | tf_op jit(solution)/shard_map/all_to_all | solution.py:115
  98.8 2.1 %reshape.303 = bf16[1152,192]{1,0:T(8,128)(2,1)} reshape(bf16[4,8,36,192]{3,2,1,0:T(8,128)(2,1)} %copy.101) | data formatting | bytes 884736 | tf_op jit(solution)/shard_map/reshape | solution.py:134
  101.0 2.4 %fusion.2 = f32[192,512]{1,0:T(8,128)} fusion(bf16[1152,192]{1,0:T(8,128)(2,1)} %reshape.303, s32[512]{0:T(512)S(1)} %multiply_add_fusion), kind=kOutput, calls=%fused_computation.11 | convolution fusion | flops 227082240 | bytes 837632 | tf_op jit(solution)/shard_map/dot_general | solution.py:24
  103.4 1.5 %multiply_reduce_fusion.2 = f32[256]{0:T(256)S(1)} fusion(bf16[256,2048]{1,0:T(8,128)(2,1)} %all-gather.2.cloned.1.call-done), kind=kLoop, calls=%fused_computation.12 | loop fusion | flops 1572608 | bytes 1049600 | tf_op jit(solution)/shard_map/reduce_sum | solution.py:14
  104.9 2.2 %fusion.4 = bf16[256,768]{1,0:T(8,128)(2,1)S(1)} fusion(bf16[256,2048]{1,0:T(8,128)(2,1)} %all-gather.2.cloned.1.call-done, bf16[768,2048]{1,0:T(8,128)(2,1)S(1)} %copy-done, f32[256]{0:T(256)S(1)} %broadcast_add_fusion), kind=kOutput, calls=%fused_computation.15 | convolution fusion | flops 805699584 | bytes 4588544 | tf_op jit(solution)/shard_map/dot_general | solution.py:11
  107.2 9.9 %gather_fusion.1 = bf16[1152]{0:T(1024)(128)(2,1)S(1)} fusion(bf16[256,768]{1,0:T(8,128)(2,1)S(1)} %fusion.4, s32[1152]{0:T(1024)S(1)} %fusion.12), kind=kCustom, calls=%fused_computation.1 | custom fusion | bytes 13824 | tf_op jit(solution)/shard_map/gather | solution.py:113
  117.8 3.3 %all-to-all-start.6 = ((bf16[4,8,36]{2,0,1:T(4,128)(2,1)}), bf16[4,8,36]{2,0,1:T(4,128)(2,1)S(1)}, u32[]{:S(2)}, u32[]{:S(2)}) async-start(bf16[4,8,36]{2,0,1:T(4,128)(2,1)} %copy.111), calls=%async_computation.6 | async-start | bytes 16384 | tf_op jit(solution)/shard_map/all_to_all | solution.py:125
  121.2 1.8 %fusion.24 = (f32[48,512]{1,0:T(8,128)}, f32[48,512]{1,0:T(8,128)}, f32[48,512]{1,0:T(8,128)}, f32[48,512]{1,0:T(8,128)}) fusion(f32[192,512]{1,0:T(8,128)} %fusion.2), kind=kLoop, calls=%fused_computation.60 | loop fusion | bytes 786432 | tf_op jit(solution)/shard_map/slice | solution.py:54
  122.9 3.8 %all-to-all-done.6 = bf16[4,8,36]{2,0,1:T(4,128)(2,1)S(1)} async-done(((bf16[4,8,36]{2,0,1:T(4,128)(2,1)}), bf16[4,8,36]{2,0,1:T(4,128)(2,1)S(1)}, u32[]{:S(2)}, u32[]{:S(2)}) %all-to-all-start.6) | async-done | bytes 2336 | tf_op jit(solution)/shard_map/all_to_all | solution.py:125
  127.4 3.2 %all-to-all-start.7 = ((bf16[4,2,144]{2,1,0:T(2,128)(2,1)}), bf16[4,2,144]{2,1,0:T(2,128)(2,1)S(1)}, u32[]{:S(2)}, u32[]{:S(2)}) async-start(bf16[4,2,144]{2,1,0:T(2,128)(2,1)} %reshape.362), calls=%async_computation.7 | async-start | bytes 8192 | tf_op jit(solution)/shard_map/all_to_all | solution.py:124
  130.6 5.8 %multiply_reduce_fusion = (f32[512]{0:T(512)S(1)}, f32[512]{0:T(512)S(1)}) fusion(f32[48,512]{1,0:T(8,128)} %get-tuple-element.7, f32[48,512]{1,0:T(8,128)} %get-tuple-element.8, f32[48,512]{1,0:T(8,128)} %get-tuple-element.9, f32[48,512]{1,0:T(8,128)} %get-tuple-element.6, f32[48,512]{1,0:T(8,128)} %broadcast_in_dim.56, f32[48,512]{1,0:T(8,128)} %broadcast_in_dim.54, ...), kind=kLoop, calls=%fused_computation.5 | loop fusion | flops 28310528 | bytes 790528 | tf_op jit(solution)/shard_map/reduce_sum | solution.py:53
  136.9 3.3 %gather_fusion.2 = f32[512]{0:T(512)S(1)} fusion(f32[1152]{0:T(1024)S(1)} %reshape.310, s32[1024]{0:T(1024)} %pad_clamp_fusion), kind=kCustom, calls=%fused_computation.2 | custom fusion | bytes 6144 | tf_op jit(solution)/shard_map/gather | solution.py:138
  140.2 1.3 fusion.14
  (71 shorter events, 15.8 us)
Async XLA Ops:
  7.2 97.8 %copy-start = (bf16[768,2048]{1,0:T(8,128)(2,1)S(1)}, bf16[768,2048]{1,0:T(8,128)(2,1)}, u32[]{:S(2)}) copy-start(bf16[768,2048]{1,0:T(8,128)(2,1)} %param.8) | copy-start | bytes 9437188
  16.1 11.9 %all-to-all-start = ((s32[8,1,144]{2,1,0:T(1,128)}), s32[8,1,144]{2,1,0:T(1,128)S(1)}, u32[]{:S(2)}, u32[]{:S(2)}) async-start(s32[8,1,144]{2,1,0:T(1,128)} %reshape.354), calls=%async_computation | async-start | bytes 16384 | tf_op jit(solution)/shard_map/all_to_all | solution.py:95
  22.4 81.0 %all-gather.2.cloned.1.call-start = ((), (), s32[]{:S(2)}) async-start(), calls=%async_computation.8 | async-start | bytes 1179648 | tf_op jit(solution)/shard_map/all_gather | solution.py:75
  29.9 8.4 %all-to-all-start.1 = ((s32[4,1,288]{2,1,0:T(1,128)}), s32[4,1,288]{2,1,0:T(1,128)S(1)}, u32[]{:S(2)}, u32[]{:S(2)}) async-start(s32[4,1,288]{2,1,0:T(1,128)} %reshape.356), calls=%async_computation.1 | async-start | bytes 12288 | tf_op jit(solution)/shard_map/all_to_all | solution.py:94
  38.3 14.2 %all-to-all-start.4 = ((s32[8,1,144]{2,1,0:T(1,128)}), s32[8,1,144]{2,1,0:T(1,128)S(1)}, u32[]{:S(2)}, u32[]{:S(2)}) async-start(s32[8,1,144]{2,1,0:T(1,128)} %reshape.358), calls=%async_computation.4 | async-start | bytes 16384 | tf_op jit(solution)/shard_map/all_to_all | solution.py:102
  42.6 15.0 %copy-start.2 = (f32[8,192]{1,0:T(8,128)S(1)}, f32[8,192]{1,0:T(8,128)}, u32[]{:S(2)}) copy-start(f32[8,192]{1,0:T(8,128)} %param.9) | copy-start | bytes 18436
  52.5 21.9 %all-to-all-start.2 = ((bf16[4,8,36,192]{3,0,2,1:T(4,128)(2,1)}), bf16[4,8,36,192]{3,0,2,1:T(4,128)(2,1)}, u32[]{:S(2)}, u32[]{:S(2)}) async-start(bf16[4,8,36,192]{3,0,2,1:T(4,128)(2,1)} %copy.99), calls=%async_computation.2 | async-start | bytes 1179648 | tf_op jit(solution)/shard_map/all_to_all | solution.py:116
  74.4 9.3 %all-to-all-start.5 = ((s32[4,1,288]{2,1,0:T(1,128)}), s32[4,1,288]{2,1,0:T(1,128)S(1)}, u32[]{:S(2)}, u32[]{:S(2)}) async-start(s32[4,1,288]{2,1,0:T(1,128)} %reshape.360), calls=%async_computation.5 | async-start | bytes 12288 | tf_op jit(solution)/shard_map/all_to_all | solution.py:101
  83.8 13.0 %all-to-all-start.3 = ((bf16[4,8,36,192]{3,1,2,0:T(8,128)(2,1)}), bf16[4,8,36,192]{3,1,2,0:T(8,128)(2,1)}, u32[]{:S(2)}, u32[]{:S(2)}) async-start(bf16[4,8,36,192]{3,1,2,0:T(8,128)(2,1)} %copy.100), calls=%async_computation.3 | async-start | bytes 1179648 | tf_op jit(solution)/shard_map/all_to_all | solution.py:115
  107.2 29.3 %copy-start.1 = (bf16[256,768]{1,0:T(8,128)(2,1)}, bf16[256,768]{1,0:T(8,128)(2,1)S(1)}, u32[]{:S(2)}) copy-start(bf16[256,768]{1,0:T(8,128)(2,1)S(1)} %fusion.4) | copy-start | bytes 1179652
  117.8 8.9 %all-to-all-start.6 = ((bf16[4,8,36]{2,0,1:T(4,128)(2,1)}), bf16[4,8,36]{2,0,1:T(4,128)(2,1)S(1)}, u32[]{:S(2)}, u32[]{:S(2)}) async-start(bf16[4,8,36]{2,0,1:T(4,128)(2,1)} %copy.111), calls=%async_computation.6 | async-start | bytes 16384 | tf_op jit(solution)/shard_map/all_to_all | solution.py:125
  127.4 9.3 %all-to-all-start.7 = ((bf16[4,2,144]{2,1,0:T(2,128)(2,1)}), bf16[4,2,144]{2,1,0:T(2,128)(2,1)S(1)}, u32[]{:S(2)}, u32[]{:S(2)}) async-start(bf16[4,2,144]{2,1,0:T(2,128)(2,1)} %reshape.362), calls=%async_computation.7 | async-start | bytes 8192 | tf_op jit(solution)/shard_map/all_to_all | solution.py:124
  130.6 9.6 %copy-start.3 = (f32[8]{0:T(128)S(1)}, f32[8]{0:T(128)}, u32[]{:S(2)}) copy-start(f32[8]{0:T(128)} %multiply_reduce_fusion.3) | copy-start | bytes 100
Sparse Core Ops, SparseCore 0:
  24.8 23.5 all-gather.1
where the time goes:
time: 150 us; the launch traced here: 148 us
  local copies, waits for them, and re-layouts  47.7 us (32%)
  waiting for transfers between devices  32.6 us (22%)
  starting transfers between devices  32.4 us (22%)
  between operations  14.3 us (10%)
  other arithmetic  13.2 us (9%)
  matrix products  8.09 us (5%)
    all_to_all x1, waiting for transfers between devices, body(): lax.all_to_all(fetched.astype(jnp.bfloat16), 'qry', split_axis=1, concat_...  14.1 us
    gather x3, local copies, waits for them, and re-layouts, body(): tversky[got_query.reshape(-1), flat_slots].astype(jnp.float32)  10.6 us
    all_to_all x1, waiting for transfers between devices, body(): lax.all_to_all(lax.all_to_all(fetched.astype(jnp.bfloat16), 'qry', split_...  7.83 us
    reduce_sum x2, other arithmetic, intersection(): jnp.sum(first[3][:, None, :] * second[3][None, :, :] * jnp.exp(-SHARPNESS...  6.76 us
    convert_element_type x3, local copies, waits for them, and re-layouts, body(): fetched.astype(jnp.bfloat16)  6.56 us
    all_to_all x1, starting transfers between devices, body(): lax.all_to_all(send_slot, 'qry', split_axis=1, concat_axis=1, tiled=True)  6.33 us
    all_to_all x1, starting transfers between devices, body(): lax.all_to_all(fetched.astype(jnp.bfloat16), 'qry', split_axis=1, concat_...  5.03 us
    all_to_all x1, waiting for transfers between devices, body(): lax.all_to_all(send_slot, 'qry', split_axis=1, concat_axis=1, tiled=True)  4.87 us
  transfers between devices with their start and end apart: 9, of which 5 were waited for; matrix products, arithmetic and copies ran while one was open for 27% of the time, Pallas kernels for 0%

commit v1 on v0

--- a/solution.py
+++ b/solution.py
@@ -113,8 +113,16 @@
     prior_all = tversky[got_query.reshape(-1), flat_slots].astype(jnp.float32).reshape(bucket_shape)
     back_atoms, back_prior = (
         lax.all_to_all(
-            lax.all_to_all(
-                fetched.astype(jnp.bfloat16), "qry", split_axis=1, concat_axis=1, tiled=True
+            jnp.concatenate(
+                lax.all_to_all(
+                    jnp.stack(
+                        jnp.split(fetched.astype(jnp.bfloat16), lax.axis_size("qry"), axis=1)
+                    ),
+                    "qry",
+                    0,
+                    0,
+                ),
+                axis=1,
             ),
             "lib",
             split_axis=0,

time: 150 us -> 156 us (1.040)
  local copies, waits for them, and re-layouts: 47.7 us -> 53.6 us
    unnamed x18 -> x25, local copies, waits for them, and re-layouts: 3.86 us -> 10.1 us
    convert_element_type x3 -> x2, local copies, waits for them, and re-layouts: 6.56 us -> 4.22 us  [body(): fetched.astype(jnp.bfloat16)]
    reshape x0 -> x1, local copies, waits for them, and re-layouts: none -> 2.07 us  [body(): jnp.concatenate(lax.all_to_all(jnp.stack(jnp.split(fetched.astype(jnp.bfl...]
    all_to_all x2 -> x1, local copies, waits for them, and re-layouts: 4.11 us -> 2.04 us  [body(): lax.all_to_all(jnp.concatenate(lax.all_to_all(jnp.stack(jnp.split(fetched...]
    another operation x0 -> x2, local copies, waits for them, and re-layouts: none -> 1.94 us  [body(): jnp.stack(jnp.split(fetched.astype(jnp.bfloat16), lax.axis_size('qry'), a...]
  transfers between devices with their start and end apart: 9 -> 9, of which waited for: 5 -> 5; matrix products, arithmetic and copies ran while one was open for 27% -> 30% of each run, Pallas kernels for 0% -> 0%
where the time goes in v1:
time: 156 us; the launch traced here: 154 us
  local copies, waits for them, and re-layouts  53.6 us (34%)
  waiting for transfers between devices  32.6 us (21%)
  starting transfers between devices  32.4 us (21%)
  between operations  14.3 us (9%)
  other arithmetic  13.2 us (8%)
  matrix products  8.09 us (5%)
    all_to_all x1, waiting for transfers between devices, body(): lax.all_to_all(jnp.stack(jnp.split(fetched.astype(jnp.bfloat16), lax.axis...  14.1 us
    gather x3, local copies, waits for them, and re-layouts, body(): tversky[got_query.reshape(-1), flat_slots].astype(jnp.float32)  10.6 us
    unnamed x25, local copies, waits for them, and re-layouts  10.1 us
    all_to_all x1, waiting for transfers between devices, body(): lax.all_to_all(jnp.concatenate(lax.all_to_all(jnp.stack(jnp.split(fetched...  7.83 us
    reduce_sum x2, other arithmetic, intersection(): jnp.sum(first[3][:, None, :] * second[3][None, :, :] * jnp.exp(-SHARPNESS...  6.76 us
    all_to_all x1, starting transfers between devices, body(): lax.all_to_all(send_slot, 'qry', split_axis=1, concat_axis=1, tiled=True)  6.33 us
    all_to_all x1, starting transfers between devices, body(): lax.all_to_all(jnp.stack(jnp.split(fetched.astype(jnp.bfloat16), lax.axis...  5.03 us
    all_to_all x1, waiting for transfers between devices, body(): lax.all_to_all(send_slot, 'qry', split_axis=1, concat_axis=1, tiled=True)  4.87 us
  transfers between devices with their start and end apart: 9, of which 5 were waited for; matrix products, arithmetic and copies ran while one was open for 30% of the time, Pallas kernels for 0%

profile of v1, /device:TPU:0, one launch (start us, length us, event | category | flops | bytes accessed | tf_op | source)
XLA Modules:
  0.0 154.2 jit_solution(11124189556459069272)
XLA Ops:
  8.9 3.6 %gather_fusion = s32[512]{0:T(512)S(1)} fusion(s32[24576]{0:T(1024)} %param.13, s32[1024]{0:T(1024)S(1)} %pad_clamp_fusion.1), kind=kCustom, calls=%fused_computation | custom fusion | bytes 6144 | tf_op jit(solution)/shard_map/jit(_take)/gather | solution.py:76
  12.8 2.5 %scatter_custom_fusion = s32[1152]{0:T(1024)S(1)} fusion(s32[512]{0:T(512)S(1)} %bitcast.84, s32[512]{0:T(512)S(1)} %get-tuple-element.4, s32[]{:T(128)} %constant.31.clone.1), kind=kCustom, calls=%fused_computation.60 | custom fusion | bytes 4612 | tf_op jit(solution)/shard_map/scatter | solution.py:88
  16.1 6.3 %all-to-all-start = ((s32[8,1,144]{2,1,0:T(1,128)}), s32[8,1,144]{2,1,0:T(1,128)S(1)}, u32[]{:S(2)}, u32[]{:S(2)}) async-start(s32[8,1,144]{2,1,0:T(1,128)} %reshape.362), calls=%async_computation | async-start | bytes 16384 | tf_op jit(solution)/shard_map/all_to_all | solution.py:95
  23.1 4.9 %all-to-all-done = s32[8,1,144]{2,1,0:T(1,128)S(1)} async-done(((s32[8,1,144]{2,1,0:T(1,128)}), s32[8,1,144]{2,1,0:T(1,128)S(1)}, u32[]{:S(2)}, u32[]{:S(2)}) %all-to-all-start) | async-done | bytes 4640 | tf_op jit(solution)/shard_map/all_to_all | solution.py:95
  29.9 3.7 %all-to-all-start.1 = ((s32[4,1,288]{2,1,0:T(1,128)}), s32[4,1,288]{2,1,0:T(1,128)S(1)}, u32[]{:S(2)}, u32[]{:S(2)}) async-start(s32[4,1,288]{2,1,0:T(1,128)} %reshape.364), calls=%async_computation.1 | async-start | bytes 12288 | tf_op jit(solution)/shard_map/all_to_all | solution.py:94
  33.7 2.4 %scatter_custom_fusion.1 = s32[1152]{0:T(1024)S(1)} fusion(s32[512]{0:T(512)S(1)} %bitcast.85, s32[512]{0:T(512)S(1)} %fusion.27, s32[]{:T(128)} %constant.31.clone.1), kind=kCustom, calls=%fused_computation.58 | custom fusion | bytes 4612 | tf_op jit(solution)/shard_map/scatter | solution.py:91
  36.9 1.4 all-to-all-done.1
  38.3 3.3 %all-to-all-start.4 = ((s32[8,1,144]{2,1,0:T(1,128)}), s32[8,1,144]{2,1,0:T(1,128)S(1)}, u32[]{:S(2)}, u32[]{:S(2)}) async-start(s32[8,1,144]{2,1,0:T(1,128)} %reshape.366), calls=%async_computation.4 | async-start | bytes 16384 | tf_op jit(solution)/shard_map/all_to_all | solution.py:102
  42.6 3.4 %fusion.1 = bf16[1152,192]{0,1:T(8,128)(2,1)} fusion(f32[768,192]{0,1:T(8,128)} %param.10, s32[1152]{0:T(1024)S(1)} %eq.45), kind=kOutput, calls=%fused_computation.9 | convolution fusion | flops 2039537664 | bytes 1036800 | tf_op jit(solution)/shard_map/dot_general | solution.py:36
  46.0 2.1 %copy.138 = bf16[1152,192]{1,0:T(8,128)(2,1)} copy(bf16[1152,192]{0,1:T(8,128)(2,1)} %fusion.1) | data formatting | bytes 884736 | tf_op jit(solution)/shard_map/convert_element_type | solution.py:119
  48.0 2.1 %convert_element_type.26 = bf16[4,8,36,192]{3,2,1,0:T(8,128)(2,1)} reshape(bf16[1152,192]{1,0:T(8,128)(2,1)} %copy.138) | data formatting | bytes 884736 | tf_op jit(solution)/shard_map/convert_element_type | solution.py:119
  57.3 1.0 copy.147
  58.4 5.0 %all-to-all-start.2 = ((bf16[8,4,1,36,192]{4,1,3,2,0:T(4,128)(2,1)}), bf16[8,4,1,36,192]{4,1,3,2,0:T(4,128)(2,1)}, u32[]{:S(2)}, u32[]{:S(2)}) async-start(bf16[8,4,1,36,192]{4,1,3,2,0:T(4,128)(2,1)} %copy.147), calls=%async_computation.2 | async-start | bytes 1179648 | tf_op jit(solution)/shard_map/all_to_all | solution.py:117
  63.8 0.9 multiply_reduce_fusion.3
  66.2 14.1 %all-to-all-done.2 = bf16[8,4,1,36,192]{4,1,3,2,0:T(4,128)(2,1)} async-done(((bf16[8,4,1,36,192]{4,1,3,2,0:T(4,128)(2,1)}), bf16[8,4,1,36,192]{4,1,3,2,0:T(4,128)(2,1)}, u32[]{:S(2)}, u32[]{:S(2)}) %all-to-all-start.2) | async-done | bytes 442400 | tf_op jit(solution)/shard_map/all_to_all | solution.py:117
  80.3 3.2 %all-to-all-start.5 = ((s32[4,1,288]{2,1,0:T(1,128)}), s32[4,1,288]{2,1,0:T(1,128)S(1)}, u32[]{:S(2)}, u32[]{:S(2)}) async-start(s32[4,1,288]{2,1,0:T(1,128)} %reshape.368), calls=%async_computation.5 | async-start | bytes 12288 | tf_op jit(solution)/shard_map/all_to_all | solution.py:101
  87.5 2.1 %copy.148 = bf16[4,8,36,192]{3,1,2,0:T(8,128)(2,1)} copy(bf16[4,8,36,192]{3,0,2,1:T(4,128)(2,1)} %bitcast.15) | data formatting | bytes 884736 | tf_op jit(solution)/shard_map/reshape | solution.py:116
  89.6 4.2 %all-to-all-start.3 = ((bf16[4,8,36,192]{3,1,2,0:T(8,128)(2,1)}), bf16[4,8,36,192]{3,1,2,0:T(8,128)(2,1)}, u32[]{:S(2)}, u32[]{:S(2)}) async-start(bf16[4,8,36,192]{3,1,2,0:T(8,128)(2,1)} %copy.148), calls=%async_computation.3 | async-start | bytes 1179648 | tf_op jit(solution)/shard_map/all_to_all | solution.py:115
  94.8 7.8 %all-to-all-done.3 = bf16[4,8,36,192]{3,1,2,0:T(8,128)(2,1)} async-done(((bf16[4,8,36,192]{3,1,2,0:T(8,128)(2,1)}), bf16[4,8,36,192]{3,1,2,0:T(8,128)(2,1)}, u32[]{:S(2)}, u32[]{:S(2)}) %all-to-all-start.3) | async-done | bytes 442400 | tf_op jit(solution)/shard_map/all_to_all | solution.py:115
  102.6 2.0 %copy.149 = bf16[4,8,36,192]{3,2,1,0:T(8,128)(2,1)} copy(bf16[4,8,36,192]{3,1,2,0:T(8,128)(2,1)} %all-to-all-done.3) | data formatting | bytes 884736 | tf_op jit(solution)/shard_map/all_to_all | solution.py:115
  104.7 2.1 %reshape.311 = bf16[1152,192]{1,0:T(8,128)(2,1)} reshape(bf16[4,8,36,192]{3,2,1,0:T(8,128)(2,1)} %copy.149) | data formatting | bytes 884736 | tf_op jit(solution)/shard_map/reshape | solution.py:142
  106.8 2.4 %fusion.2 = f32[192,512]{1,0:T(8,128)} fusion(bf16[1152,192]{1,0:T(8,128)(2,1)} %reshape.311, s32[512]{0:T(512)S(1)} %multiply_add_fusion), kind=kOutput, calls=%fused_computation.11 | convolution fusion | flops 227082240 | bytes 837632 | tf_op jit(solution)/shard_map/dot_general | solution.py:24
  109.2 1.5 multiply_reduce_fusion.2
  110.8 2.2 %fusion.4 = bf16[256,768]{1,0:T(8,128)(2,1)S(1)} fusion(bf16[256,2048]{1,0:T(8,128)(2,1)} %all-gather.2.cloned.1.call-done, bf16[768,2048]{1,0:T(8,128)(2,1)S(1)} %copy-done, f32[256]{0:T(256)S(1)} %broadcast_add_fusion), kind=kOutput, calls=%fused_computation.15 | convolution fusion | flops 805699584 | bytes 4588544 | tf_op jit(solution)/shard_map/dot_general | solution.py:11
  113.0 9.9 %gather_fusion.1 = bf16[1152]{0:T(1024)(128)(2,1)S(1)} fusion(bf16[256,768]{1,0:T(8,128)(2,1)S(1)} %fusion.4, s32[1152]{0:T(1024)S(1)} %fusion.20), kind=kCustom, calls=%fused_computation.1 | custom fusion | bytes 13824 | tf_op jit(solution)/shard_map/gather | solution.py:113
  123.7 3.3 %all-to-all-start.6 = ((bf16[4,8,36]{2,0,1:T(4,128)(2,1)}), bf16[4,8,36]{2,0,1:T(4,128)(2,1)S(1)}, u32[]{:S(2)}, u32[]{:S(2)}) async-start(bf16[4,8,36]{2,0,1:T(4,128)(2,1)} %copy.159), calls=%async_computation.6 | async-start | bytes 16384 | tf_op jit(solution)/shard_map/all_to_all | solution.py:133
  127.0 1.8 %fusion.32 = (f32[48,512]{1,0:T(8,128)}, f32[48,512]{1,0:T(8,128)}, f32[48,512]{1,0:T(8,128)}, f32[48,512]{1,0:T(8,128)}) fusion(f32[192,512]{1,0:T(8,128)} %fusion.2), kind=kLoop, calls=%fused_computation.76 | loop fusion | bytes 786432 | tf_op jit(solution)/shard_map/slice | solution.py:54
  128.8 3.8 %all-to-all-done.6 = bf16[4,8,36]{2,0,1:T(4,128)(2,1)S(1)} async-done(((bf16[4,8,36]{2,0,1:T(4,128)(2,1)}), bf16[4,8,36]{2,0,1:T(4,128)(2,1)S(1)}, u32[]{:S(2)}, u32[]{:S(2)}) %all-to-all-start.6) | async-done | bytes 2336 | tf_op jit(solution)/shard_map/all_to_all | solution.py:133
  133.2 3.2 %all-to-all-start.7 = ((bf16[4,2,144]{2,1,0:T(2,128)(2,1)}), bf16[4,2,144]{2,1,0:T(2,128)(2,1)S(1)}, u32[]{:S(2)}, u32[]{:S(2)}) async-start(bf16[4,2,144]{2,1,0:T(2,128)(2,1)} %reshape.370), calls=%async_computation.7 | async-start | bytes 8192 | tf_op jit(solution)/shard_map/all_to_all | solution.py:132
  136.5 5.8 %multiply_reduce_fusion = (f32[512]{0:T(512)S(1)}, f32[512]{0:T(512)S(1)}) fusion(f32[48,512]{1,0:T(8,128)} %get-tuple-element.7, f32[48,512]{1,0:T(8,128)} %get-tuple-element.8, f32[48,512]{1,0:T(8,128)} %get-tuple-element.9, f32[48,512]{1,0:T(8,128)} %get-tuple-element.6, f32[48,512]{1,0:T(8,128)} %broadcast_in_dim.56, f32[48,512]{1,0:T(8,128)} %broadcast_in_dim.54, ...), kind=kLoop, calls=%fused_computation.5 | loop fusion | flops 28310528 | bytes 790528 | tf_op jit(solution)/shard_map/reduce_sum | solution.py:53
  142.7 3.3 %gather_fusion.2 = f32[512]{0:T(512)S(1)} fusion(f32[1152]{0:T(1024)S(1)} %reshape.318, s32[1024]{0:T(1024)} %pad_clamp_fusion), kind=kCustom, calls=%fused_computation.2 | custom fusion | bytes 6144 | tf_op jit(solution)/shard_map/gather | solution.py:146
  146.1 1.3 fusion.22
  (79 shorter events, 23.0 us)
Async XLA Ops:
  7.2 103.6 %copy-start = (bf16[768,2048]{1,0:T(8,128)(2,1)S(1)}, bf16[768,2048]{1,0:T(8,128)(2,1)}, u32[]{:S(2)}) copy-start(bf16[768,2048]{1,0:T(8,128)(2,1)} %param.8) | copy-start | bytes 9437188
  16.1 11.9 %all-to-all-start = ((s32[8,1,144]{2,1,0:T(1,128)}), s32[8,1,144]{2,1,0:T(1,128)S(1)}, u32[]{:S(2)}, u32[]{:S(2)}) async-start(s32[8,1,144]{2,1,0:T(1,128)} %reshape.362), calls=%async_computation | async-start | bytes 16384 | tf_op jit(solution)/shard_map/all_to_all | solution.py:95
  22.4 86.9 %all-gather.2.cloned.1.call-start = ((), (), s32[]{:S(2)}) async-start(), calls=%async_computation.8 | async-start | bytes 1179648 | tf_op jit(solution)/shard_map/all_gather | solution.py:75
  29.9 8.4 %all-to-all-start.1 = ((s32[4,1,288]{2,1,0:T(1,128)}), s32[4,1,288]{2,1,0:T(1,128)S(1)}, u32[]{:S(2)}, u32[]{:S(2)}) async-start(s32[4,1,288]{2,1,0:T(1,128)} %reshape.364), calls=%async_computation.1 | async-start | bytes 12288 | tf_op jit(solution)/shard_map/all_to_all | solution.py:94
  38.3 20.0 %all-to-all-start.4 = ((s32[8,1,144]{2,1,0:T(1,128)}), s32[8,1,144]{2,1,0:T(1,128)S(1)}, u32[]{:S(2)}, u32[]{:S(2)}) async-start(s32[8,1,144]{2,1,0:T(1,128)} %reshape.366), calls=%async_computation.4 | async-start | bytes 16384 | tf_op jit(solution)/shard_map/all_to_all | solution.py:102
  46.0 17.5 %copy-start.2 = (f32[8,192]{1,0:T(8,128)S(1)}, f32[8,192]{1,0:T(8,128)}, u32[]{:S(2)}) copy-start(f32[8,192]{1,0:T(8,128)} %param.9) | copy-start | bytes 18436
  58.4 21.9 %all-to-all-start.2 = ((bf16[8,4,1,36,192]{4,1,3,2,0:T(4,128)(2,1)}), bf16[8,4,1,36,192]{4,1,3,2,0:T(4,128)(2,1)}, u32[]{:S(2)}, u32[]{:S(2)}) async-start(bf16[8,4,1,36,192]{4,1,3,2,0:T(4,128)(2,1)} %copy.147), calls=%async_computation.2 | async-start | bytes 1179648 | tf_op jit(solution)/shard_map/all_to_all | solution.py:117
  80.3 9.3 %all-to-all-start.5 = ((s32[4,1,288]{2,1,0:T(1,128)}), s32[4,1,288]{2,1,0:T(1,128)S(1)}, u32[]{:S(2)}, u32[]{:S(2)}) async-start(s32[4,1,288]{2,1,0:T(1,128)} %reshape.368), calls=%async_computation.5 | async-start | bytes 12288 | tf_op jit(solution)/shard_map/all_to_all | solution.py:101
  89.6 13.0 %all-to-all-start.3 = ((bf16[4,8,36,192]{3,1,2,0:T(8,128)(2,1)}), bf16[4,8,36,192]{3,1,2,0:T(8,128)(2,1)}, u32[]{:S(2)}, u32[]{:S(2)}) async-start(bf16[4,8,36,192]{3,1,2,0:T(8,128)(2,1)} %copy.148), calls=%async_computation.3 | async-start | bytes 1179648 | tf_op jit(solution)/shard_map/all_to_all | solution.py:115
  113.0 29.3 %copy-start.1 = (bf16[256,768]{1,0:T(8,128)(2,1)}, bf16[256,768]{1,0:T(8,128)(2,1)S(1)}, u32[]{:S(2)}) copy-start(bf16[256,768]{1,0:T(8,128)(2,1)S(1)} %fusion.4) | copy-start | bytes 1179652
  123.7 8.9 %all-to-all-start.6 = ((bf16[4,8,36]{2,0,1:T(4,128)(2,1)}), bf16[4,8,36]{2,0,1:T(4,128)(2,1)S(1)}, u32[]{:S(2)}, u32[]{:S(2)}) async-start(bf16[4,8,36]{2,0,1:T(4,128)(2,1)} %copy.159), calls=%async_computation.6 | async-start | bytes 16384 | tf_op jit(solution)/shard_map/all_to_all | solution.py:133
  133.2 9.3 %all-to-all-start.7 = ((bf16[4,2,144]{2,1,0:T(2,128)(2,1)}), bf16[4,2,144]{2,1,0:T(2,128)(2,1)S(1)}, u32[]{:S(2)}, u32[]{:S(2)}) async-start(bf16[4,2,144]{2,1,0:T(2,128)(2,1)} %reshape.370), calls=%async_computation.7 | async-start | bytes 8192 | tf_op jit(solution)/shard_map/all_to_all | solution.py:132
  136.5 9.6 %copy-start.3 = (f32[8]{0:T(128)S(1)}, f32[8]{0:T(128)}, u32[]{:S(2)}) copy-start(f32[8]{0:T(128)} %multiply_reduce_fusion.3) | copy-start | bytes 100
Sparse Core Ops, SparseCore 0:
  24.8 23.5 all-gather.1
